TPU v7x, 32 devices: a whole 2x2x4 slice. The times are simulated.
32 devices in a mesh: gx: 2 (over y), gy: 4 (over x, core), gz: 4 (over z).
Axes of the slice: x: 2, y: 2, z: 4, core: 2. Of those that a mesh axis runs over, the one named last changes fastest.
Arguments:
- features: bfloat16 [24576, 256], P(('gx', 'gy', 'gz')), may hold values from -6 to 6
- tile_values: bfloat16 [256, 8, 128, 128], P(('gx', 'gy', 'gz')), as said below
- tile_columns: int32 [256, 8], P(('gx', 'gy', 'gz')), may hold values from 0 to 7
- tile_present: int32 [256, 8], P(('gx', 'gy', 'gz')), may hold values 0 or 1
- host_root: int32 [64], P(('gx', 'gy')), may hold values from 0 to 3, as said below
- host_block: int32 [64], P(('gx', 'gy')), may hold values from 0 to 1
- self_one: bfloat16 [256, 256], replicated, may hold values from -0.375 to 0.375
- neigh_one: bfloat16 [256, 256], replicated, may hold values from -0.375 to 0.375
- scale_one: float32 [256], replicated, may hold values from 0.25 to 1.75
- shift_one: float32 [256], replicated, may hold values from -3 to 3
- self_two: bfloat16 [256, 256], replicated, may hold values from -0.375 to 0.375
- neigh_two: bfloat16 [256, 256], replicated, may hold values from -0.375 to 0.375
Outputs:
- embedding: bfloat16 [24576, 256], P(('gx', 'gy', 'gz'))
Inputs may be any that keep to these rules, and one draw needn't show every extreme that they name: `host_root`: never the holder's own gz index; the 2 replica slots of one device name 2 different devices. `tile_values`: entries lie in 0 to 1.8 / sqrt(1024).
All inputs are finite; a program needn't handle non-finite values. No bound on the sum of `tile_present` on one device may be relied on, other than what follows from the above.
Results may differ from a plain program's by a relative error of at most 0.012.
Values may be sent and summed in bfloat16 or wider, within the bound.
A program may use at most 64 MiB of HBM per device.

v0:
```python
import jax
import jax.numpy as jnp
from jax import lax
from jax.sharding import PartitionSpec as P

OWN = 4
SPLIT = 2


def per_device(
    features,
    tile_values,
    tile_columns,
    tile_present,
    host_root,
    host_block,
    self_one,
    neigh_one,
    scale_one,
    shift_one,
    self_two,
    neigh_two,
):
    tile = tile_values.shape[2]
    width = features.shape[1]
    rooted = features.shape[0] // tile
    slots = tile_values.shape[0]
    hosts = slots - rooted
    group = lax.axis_size("gz")
    mine = lax.axis_index("gz")
    root_table = host_root.reshape(group, hosts)
    block_table = host_block.reshape(group, hosts)
    my_roots = lax.dynamic_index_in_dim(root_table, mine, 0, keepdims=False)
    peers = jnp.arange(group, dtype=jnp.int32)
    splits = jnp.arange(SPLIT, dtype=jnp.int32)
    matched = (root_table == mine)[:, :, None] & (block_table[:, :, None] == splits[None, None, :])
    holders = jnp.sum(matched.astype(jnp.int32), axis=1).astype(jnp.bfloat16)
    routing = (my_roots[:, None] == peers[None, :]).astype(jnp.bfloat16)

    def spread(rows):
        split_rows = rows.reshape(rooted, tile, width)[OWN:]
        outgoing = jnp.einsum(
            "qs,sif->qif", holders, split_rows, preferred_element_type=jnp.float32
        ).astype(jnp.bfloat16)
        incoming = lax.all_to_all(outgoing, "gz", split_axis=0, concat_axis=0, tiled=True)
        return incoming[my_roots]

    def collect(replica_partial):
        outgoing = jnp.einsum(
            "hq,hif->qif", routing, replica_partial, preferred_element_type=jnp.float32
        ).astype(jnp.bfloat16)
        incoming = lax.all_to_all(outgoing, "gz", split_axis=0, concat_axis=0, tiled=True)
        return jnp.einsum("qs,qif->sif", holders, incoming, preferred_element_type=jnp.float32)

    def aggregate(view):
        picked = view[tile_columns]
        picked = jnp.where(tile_present[:, :, None, None] > 0, picked, jnp.zeros_like(picked))
        return jnp.einsum("bkij,bkjf->bif", tile_values, picked, preferred_element_type=jnp.float32)

    def layer(rows, w_self, w_neigh):
        hosted = spread(rows)
        view = jnp.concatenate([rows.reshape(rooted, tile, width), hosted], axis=0)
        partial_value = aggregate(view)
        remote = collect(partial_value[rooted:].astype(jnp.bfloat16))
        total = partial_value[:rooted].at[OWN:].add(remote)
        neighbours = total.astype(jnp.bfloat16).reshape(-1, width)
        return jnp.dot(rows, w_self, preferred_element_type=jnp.float32) + jnp.dot(
            neighbours, w_neigh, preferred_element_type=jnp.float32
        )

    first = layer(features, self_one, neigh_one)
    sums, squares = lax.psum(
        (jnp.sum(first, axis=0), jnp.sum(first * first, axis=0)), ("gx", "gy", "gz")
    )
    count = first.shape[0] * lax.axis_size("gx") * lax.axis_size("gy") * group
    mean = sums / count
    var = squares / count - mean * mean
    hidden = jax.nn.relu((first - mean) * lax.rsqrt(var + 1e-05) * scale_one + shift_one).astype(
        jnp.bfloat16
    )
    second = layer(hidden, self_two, neigh_two)
    return second.astype(jnp.bfloat16)


def solution(mesh):
    return jax.shard_map(
        per_device,
        mesh=mesh,
        in_specs=(
            P(("gx", "gy", "gz"), None),
            P(("gx", "gy", "gz"), None, None, None),
            P(("gx", "gy", "gz"), None),
            P(("gx", "gy", "gz"), None),
            P(("gx", "gy")),
            P(("gx", "gy")),
            P(),
            P(),
            P(),
            P(),
            P(),
            P(),
        ),
        out_specs=P(("gx", "gy", "gz"), None),
        check_vma=False,
    )
```

profile of v0, /device:TPU:0, one launch (start us, length us, event | category | flops | bytes accessed | tf_op | source)
XLA Modules:
  0.0 118.0 jit_solution(8928535711859239340)
XLA Ops:
  0.0 0.9 reshape.121
  1.0 0.7 eq.42
  1.9 0.9 slice.76
  3.1 0.7 copy.39
  3.9 6.3 %all-to-all-start = ((bf16[4,128,256]{2,1,0:T(8,128)(2,1)}), bf16[4,128,256]{2,1,0:T(8,128)(2,1)S(1)}, u32[]{:S(2)}, u32[]{:S(2)}) async-start(bf16[4,128,256]{2,1,0:T(8,128)(2,1)} %copy.39), calls=%async_computation | async-start | bytes 524288 | tf_op jit(solution)/shard_map/all_to_all | solution.py:45
  10.2 0.7 compare_select_fusion
  11.0 0.7 broadcast_compare_fusion
  11.7 7.4 %all-to-all-done = bf16[4,128,256]{2,1,0:T(8,128)(2,1)S(1)} async-done(((bf16[4,128,256]{2,1,0:T(8,128)(2,1)}), bf16[4,128,256]{2,1,0:T(8,128)(2,1)S(1)}, u32[]{:S(2)}, u32[]{:S(2)}) %all-to-all-start) | async-done | bytes 262176 | tf_op jit(solution)/shard_map/all_to_all | solution.py:45
  19.7 1.0 pad_maximum_fusion
  20.7 2.8 %gather_fusion.1 = bf16[64,128,256]{2,1,0:T(8,128)(2,1)} fusion(bf16[8,128,256]{2,1,0:T(8,128)(2,1)S(1)} %pad_maximum_fusion, s32[1024]{0:T(1024)S(1)} %pad_clamp_fusion), kind=kCustom, calls=%fused_computation.1 | custom fusion | bytes 8388864 | tf_op jit(solution)/shard_map/gather | solution.py:56
  23.5 3.2 %fusion.8 = f32[8,128,256]{2,1,0:T(8,128)S(1)} fusion(bf16[8,8,128,128]{3,2,1,0:T(8,128)(2,1)S(1)} %copy-done, bf16[8,8,128,256]{3,2,1,0:T(8,128)(2,1)} %bitcast.50, pred[8,8]{1,0:T(8,128)(4,1)S(1)} %broadcast_compare_fusion), kind=kOutput, calls=%fused_computation.12 | convolution fusion | flops 538968064 | bytes 7340096 | tf_op jit(solution)/shard_map/bkij,bkjf->bif/dot_general | solution.py:58
  26.7 1.0 copy-done.3
  28.1 0.7 copy.41
  28.8 3.4 %all-to-all-start.1 = ((bf16[4,128,256]{2,1,0:T(8,128)(2,1)}), bf16[4,128,256]{2,1,0:T(8,128)(2,1)S(1)}, u32[]{:S(2)}, u32[]{:S(2)}) async-start(bf16[4,128,256]{2,1,0:T(8,128)(2,1)} %copy.41), calls=%async_computation.1 | async-start | bytes 524288 | tf_op jit(solution)/shard_map/all_to_all | solution.py:52
  32.2 1.2 fusion.39
  33.4 1.2 slice.94
  34.6 4.6 %all-to-all-done.1 = bf16[4,128,256]{2,1,0:T(8,128)(2,1)S(1)} async-done(((bf16[4,128,256]{2,1,0:T(8,128)(2,1)}), bf16[4,128,256]{2,1,0:T(8,128)(2,1)S(1)}, u32[]{:S(2)}, u32[]{:S(2)}) %all-to-all-start.1) | async-done | bytes 262176 | tf_op jit(solution)/shard_map/all_to_all | solution.py:52
  39.5 1.0 fusion.16
  40.5 2.1 %fusion.38 = (f32[256]{0:T(256)S(1)}, f32[256]{0:T(256)S(1)}, f32[768,256]{1,0:T(8,128)}) fusion(f32[768,256]{1,0:T(8,128)S(1)} %fusion.39, bf16[768,256]{1,0:T(8,128)(2,1)S(1)} %bitcast.52, bf16[256,256]{1,0:T(8,128)(2,1)} %param.23), kind=kOutput, calls=%fused_computation.63 | convolution fusion | flops 101449216 | bytes 2099200 | tf_op jit(solution)/shard_map/dot_general | solution.py:67
  42.6 39.9 %all-reduce = (f32[256]{0:T(256)S(1)}, f32[256]{0:T(256)S(1)}) all-reduce(f32[256]{0:T(256)S(1)} %get-tuple-element.30, f32[256]{0:T(256)S(1)} %get-tuple-element.29), channel_id=1, replica_groups=mesh['gx'=2,'gy'=4,'gz'=4] {'gx','gy','gz'}, use_global_device_ids=true, to_apply=%region_4.5 | all-reduce | flops 512 | bytes 4096 | tf_op jit(solution)/shard_map/psum | solution.py:72
  82.5 1.3 %maximum_convert_fusion = bf16[768,256]{1,0:T(8,128)(2,1)S(1)} fusion(f32[768,256]{1,0:T(8,128)} %get-tuple-element.35, f32[256]{0:T(256)S(1)} %copy-done.4, f32[256]{0:T(256)} %param.24, f32[256]{0:T(256)S(1)} %get-tuple-element.34, f32[256]{0:T(256)S(1)} %get-tuple-element.33), kind=kLoop, calls=%fused_computation.21 | loop fusion | flops 1179648 | bytes 1183744 | tf_op jit(solution)/shard_map/convert_element_type | solution.py:78
  84.2 10.7 %all_to_all.20 = bf16[4,128,256]{2,1,0:T(8,128)(2,1)S(1)} all-to-all(bf16[4,128,256]{2,1,0:T(8,128)(2,1)S(1)} %copy.45), channel_id=1, replica_groups=mesh['gx'=2,'gy'=4,'gz'=4] {'gz'}, dimensions={0} | all-to-all | bytes 524288 | tf_op jit(solution)/shard_map/all_to_all | solution.py:45
  95.5 2.8 %gather_fusion.3 = bf16[64,128,256]{2,1,0:T(8,128)(2,1)} fusion(bf16[8,128,256]{2,1,0:T(8,128)(2,1)S(1)} %pad_maximum_fusion.1, s32[1024]{0:T(1024)S(1)} %pad_clamp_fusion), kind=kCustom, calls=%fused_computation.3 | custom fusion | bytes 8388864 | tf_op jit(solution)/shard_map/gather | solution.py:56
  98.3 3.1 %fusion.11 = f32[8,128,256]{2,1,0:T(8,128)S(1)} fusion(bf16[8,8,128,128]{3,2,1,0:T(8,128)(2,1)S(1)} %copy-done, bf16[8,8,128,256]{3,2,1,0:T(8,128)(2,1)} %bitcast.49, pred[8,8]{1,0:T(8,128)(4,1)S(1)} %copy-done.6), kind=kOutput, calls=%fused_computation.13 | convolution fusion | flops 538968064 | bytes 7340096 | tf_op jit(solution)/shard_map/bkij,bkjf->bif/dot_general | solution.py:58
  101.4 1.0 copy-done.2
  102.8 0.7 copy.47
  103.6 3.4 %all-to-all-start.3 = ((bf16[4,128,256]{2,1,0:T(8,128)(2,1)}), bf16[4,128,256]{2,1,0:T(8,128)(2,1)S(1)}, u32[]{:S(2)}, u32[]{:S(2)}) async-start(bf16[4,128,256]{2,1,0:T(8,128)(2,1)} %copy.47), calls=%async_computation.3 | async-start | bytes 524288 | tf_op jit(solution)/shard_map/all_to_all | solution.py:52
  107.0 1.2 fusion.40
  108.2 1.2 slice.98
  109.3 5.5 %all-to-all-done.3 = bf16[4,128,256]{2,1,0:T(8,128)(2,1)S(1)} async-done(((bf16[4,128,256]{2,1,0:T(8,128)(2,1)}), bf16[4,128,256]{2,1,0:T(8,128)(2,1)S(1)}, u32[]{:S(2)}, u32[]{:S(2)}) %all-to-all-start.3) | async-done | bytes 262176 | tf_op jit(solution)/shard_map/all_to_all | solution.py:52
  115.1 1.0 fusion.15
  116.1 1.9 %fusion.14 = bf16[768,256]{1,0:T(8,128)(2,1)} fusion(f32[768,256]{1,0:T(8,128)S(1)} %fusion.40, bf16[768,256]{1,0:T(8,128)(2,1)S(1)} %bitcast.53, bf16[256,256]{1,0:T(8,128)(2,1)} %param.27), kind=kOutput, calls=%fused_computation.16 | convolution fusion | flops 101056512 | bytes 1703936 | tf_op jit(solution)/shard_map/dot_general | solution.py:67
  (40 shorter events, 3.7 us)
Async XLA Ops:
  0.0 23.5 %copy-start = (bf16[8,8,128,128]{3,2,1,0:T(8,128)(2,1)S(1)}, bf16[8,8,128,128]{3,2,1,0:T(8,128)(2,1)}, u32[]{:S(2)}) copy-start(bf16[8,8,128,128]{3,2,1,0:T(8,128)(2,1)} %param.17) | copy-start | bytes 6291460
  3.9 15.2 %all-to-all-start = ((bf16[4,128,256]{2,1,0:T(8,128)(2,1)}), bf16[4,128,256]{2,1,0:T(8,128)(2,1)S(1)}, u32[]{:S(2)}, u32[]{:S(2)}) async-start(bf16[4,128,256]{2,1,0:T(8,128)(2,1)} %copy.39), calls=%async_computation | async-start | bytes 524288 | tf_op jit(solution)/shard_map/all_to_all | solution.py:45
  11.0 16.7 %copy-start.7 = (s32[2]{0:T(128)}, s32[2]{0:T(128)S(1)}, u32[]{:S(2)}) copy-start(s32[2]{0:T(128)S(1)} %fusion.35) | copy-start | bytes 28
  11.7 11.8 %copy-start.5 = (pred[8,8]{1,0:T(8,128)(4,1)}, pred[8,8]{1,0:T(8,128)(4,1)S(1)}, u32[]{:S(2)}) copy-start(pred[8,8]{1,0:T(8,128)(4,1)S(1)} %broadcast_compare_fusion) | copy-start | bytes 196
  23.5 8.7 %copy-start.1 = (bf16[768,256]{1,0:T(8,128)(2,1)S(1)}, bf16[768,256]{1,0:T(8,128)(2,1)}, u32[]{:S(2)}) copy-start(bf16[768,256]{1,0:T(8,128)(2,1)} %param.16) | copy-start | bytes 1179652
  26.7 1.0 copy-start.3
  27.6 54.9 %copy-start.4 = (f32[256]{0:T(256)S(1)}, f32[256]{0:T(256)}, u32[]{:S(2)}) copy-start(f32[256]{0:T(256)} %param.25) | copy-start | bytes 3076
  28.8 10.4 %all-to-all-start.1 = ((bf16[4,128,256]{2,1,0:T(8,128)(2,1)}), bf16[4,128,256]{2,1,0:T(8,128)(2,1)S(1)}, u32[]{:S(2)}, u32[]{:S(2)}) async-start(bf16[4,128,256]{2,1,0:T(8,128)(2,1)} %copy.41), calls=%async_computation.1 | async-start | bytes 524288 | tf_op jit(solution)/shard_map/all_to_all | solution.py:52
  95.5 2.8 %copy-start.6 = (pred[8,8]{1,0:T(8,128)(4,1)S(1)}, pred[8,8]{1,0:T(8,128)(4,1)}, u32[]{:S(2)}) copy-start(pred[8,8]{1,0:T(8,128)(4,1)} %copy-done.5) | copy-start | bytes 196
  98.3 4.1 %copy-start.8 = (s32[2]{0:T(128)S(1)}, s32[2]{0:T(128)}, u32[]{:S(2)}) copy-start(s32[2]{0:T(128)} %copy-done.7) | copy-start | bytes 28
  101.4 1.0 copy-start.2
  103.6 11.2 %all-to-all-start.3 = ((bf16[4,128,256]{2,1,0:T(8,128)(2,1)}), bf16[4,128,256]{2,1,0:T(8,128)(2,1)S(1)}, u32[]{:S(2)}, u32[]{:S(2)}) async-start(bf16[4,128,256]{2,1,0:T(8,128)(2,1)} %copy.47), calls=%async_computation.3 | async-start | bytes 524288 | tf_op jit(solution)/shard_map/all_to_all | solution.py:52
where the time goes:
time: 119 us; the launch traced here: 118 us
  blocking collectives  50.6 us (43%)
  waiting for transfers between devices  17.5 us (15%)
  local copies, waits for them, and re-layouts  16 us (13%)
  matrix products  14.7 us (12%)
  starting transfers between devices  13.1 us (11%)
  other arithmetic  5.78 us (5%)
    psum x1, blocking collectives, per_device(): lax.psum((jnp.sum(first, axis=0), jnp.sum(first * first, axis=0)), ('gx',...  39.9 us
    all_to_all x1, blocking collectives, spread(): lax.all_to_all(outgoing, 'gz', split_axis=0, concat_axis=0, tiled=True)  10.7 us
    all_to_all x2, waiting for transfers between devices, collect(): lax.all_to_all(outgoing, 'gz', split_axis=0, concat_axis=0, tiled=True)  10.1 us
    all_to_all x1, waiting for transfers between devices, spread(): lax.all_to_all(outgoing, 'gz', split_axis=0, concat_axis=0, tiled=True)  7.39 us
    all_to_all x2, starting transfers between devices, collect(): lax.all_to_all(outgoing, 'gz', split_axis=0, concat_axis=0, tiled=True)  6.81 us
    all_to_all x1, starting transfers between devices, spread(): lax.all_to_all(outgoing, 'gz', split_axis=0, concat_axis=0, tiled=True)  6.32 us
    dot_general x2, matrix products, aggregate(): jnp.einsum('bkij,bkjf->bif', tile_values, picked, preferred_element_type=...  6.28 us
    gather x2, local copies, waits for them, and re-layouts, aggregate(): picked = view[tile_columns]  5.52 us
  transfers between devices with their start and end apart: 3, of which 3 were waited for; matrix products, arithmetic and copies ran while one was open for 5% of the time, Pallas kernels for 0%

commit v1 on v0

v1 whole, which is shorter than its diff:
```python
import functools

import jax
import jax.numpy as jnp
from jax import lax
from jax.experimental import pallas as pl
from jax.experimental.pallas import tpu as pltpu
from jax.sharding import PartitionSpec as P

OWN = 4
SPLIT = 2
LANES = 128
F32 = jnp.float32
BF16 = jnp.bfloat16


def dot(a, b):
    return jnp.dot(a, b, preferred_element_type=F32)


def kernel(
    sizes,
    columns_ref,
    present_ref,
    root_ref,
    block_ref,
    features_hbm,
    tiles_hbm,
    self_one_hbm,
    neigh_one_hbm,
    self_two_hbm,
    neigh_two_hbm,
    scale_ref,
    shift_ref,
    out_ref,
    *scratch,
):
    nx, ny, group, slots, ks, tile, width, rooted = sizes
    hosts = slots - rooted
    rows_n = rooted * tile
    own_n = OWN * tile
    parts = width // LANES
    peers = group - 1
    scratch = list(scratch)

    def take(n):
        got = scratch[:n]
        del scratch[:n]
        return got

    feat, tiles, ws1, wn1, ws2, wn2 = take(6)
    dense, acc, first, hidden, delta = take(5)
    hosted = take(parts)
    replica = take(parts)
    f_in = [take(parts) for _ in range(2)]
    f_out = [take(parts) for _ in range(2)]
    p_in = [take(parts) for _ in range(2)]
    p_out = [take(parts) for _ in range(2)]
    z_out, z_in, xy_out, xy_in = take(4)
    local_sem, f_send, f_recv, p_send, p_recv, z_send, z_recv, xy_send, xy_recv = take(9)

    gx, gy, gz = lax.axis_index("gx"), lax.axis_index("gy"), lax.axis_index("gz")
    loads = [
        pltpu.make_async_copy(src, dst, local_sem.at[i])
        for i, (src, dst) in enumerate(
            zip(
                (features_hbm, tiles_hbm, self_one_hbm, neigh_one_hbm, self_two_hbm, neigh_two_hbm),
                (feat, tiles, ws1, wn1, ws2, wn2),
            )
        )
    ]
    for load in loads:
        load.start()

    def ahead(j):
        return lax.rem(gz + j, group)

    def behind(j):
        return lax.rem(gz + group - j, group)

    spots = [(i, k) for i in range(nx) for k in range(ny) if (i, k) != (0, 0)]

    def spot_id(spot):
        return {"gx": lax.rem(gx + spot[0], nx), "gy": lax.rem(gy + spot[1], ny)}

    barrier = pltpu.get_barrier_semaphore()
    for j in range(1, group):
        pl.semaphore_signal(
            barrier, inc=1, device_id={"gz": ahead(j)}, device_id_type=pl.DeviceIdType.MESH
        )
    for spot in spots:
        pl.semaphore_signal(
            barrier, inc=1, device_id=spot_id(spot), device_id_type=pl.DeviceIdType.MESH
        )

    def z_copy(src, dst, send, recv, j):
        return pltpu.make_async_remote_copy(
            src_ref=src,
            dst_ref=dst,
            send_sem=send,
            recv_sem=recv,
            device_id={"gz": ahead(j)},
            device_id_type=pl.DeviceIdType.MESH,
        )

    def f_copy(l, c, j):
        return z_copy(
            f_out[l][c].at[j - 1], f_in[l][c].at[j - 1], f_send.at[l, c, j - 1], f_recv.at[l, c, j - 1], j
        )

    def p_copy(l, c, j):
        return z_copy(
            p_out[l][c].at[j - 1], p_in[l][c].at[j - 1], p_send.at[l, c, j - 1], p_recv.at[l, c, j - 1], j
        )

    def zs_copy(j):
        return z_copy(z_out, z_in.at[j - 1], z_send.at[j - 1], z_recv.at[j - 1], j)

    def xy_copy(n):
        return pltpu.make_async_remote_copy(
            src_ref=xy_out,
            dst_ref=xy_in.at[n],
            send_sem=xy_send.at[n],
            recv_sem=xy_recv.at[n],
            device_id=spot_id(spots[n]),
            device_id_type=pl.DeviceIdType.MESH,
        )

    def lanes(c):
        return slice(c * LANES, (c + 1) * LANES)

    def wanted(j):
        q = ahead(j)
        sel = jnp.int32(0)
        for h in range(hosts):
            at = q * hosts + h
            sel = jnp.where(root_ref[at] == gz, block_ref[at], sel)
        return sel

    def spread(l, source, base):
        for c in range(parts):
            for j in range(1, group):
                f_out[l][c][j - 1] = source[base + wanted(j)][:, lanes(c)]
                f_copy(l, c, j).start()

    loads[0].wait()
    pl.semaphore_wait(barrier, peers + len(spots))
    spread(0, feat, OWN)

    loads[1].wait()

    def build(b, carry):
        at = pl.multiple_of(b * tile, tile)
        for c in range(slots):
            total = jnp.zeros((tile, tile), BF16)
            for k in range(ks):
                on = (columns_ref[b, k] == c) & (present_ref[b, k] > 0)
                total = total + jnp.where(on, tiles[b, k], jnp.zeros((tile, tile), BF16))
            dense[pl.ds(at, tile), c * tile : (c + 1) * tile] = total
        return carry

    lax.fori_loop(0, slots, build, 0)
    for load in loads[2:]:
        load.wait()

    def blocks_of(n):
        return 2 * tile if n % (2 * tile) == 0 else tile

    def layer(l, rows, hosted_block, w_self, w_neigh, emit):
        flat = rows.reshape(rows_n, width)
        step = blocks_of(slots * tile)

        def local(i, carry):
            at = pl.multiple_of(i * step, step)
            acc[pl.ds(at, step), :] = dot(dense[pl.ds(at, step), 0:rows_n], flat[...])
            return carry

        lax.fori_loop(0, slots * tile // step, local, 0)

        for c in range(parts):
            for j in range(1, group):
                f_copy(l, c, j).wait_recv()
            for h in range(hosts):
                root = root_ref[gz * hosts + h]
                at = jnp.maximum(lax.rem(gz - root + group, group) - 1, 0)
                hosted[c][h * tile : (h + 1) * tile, :] = hosted_block(f_in[l][c][at], at, c)
            part = acc[rows_n:, lanes(c)] + dot(dense[rows_n:, rows_n:], hosted[c][...])
            replica[c][...] = part.astype(BF16).reshape(hosts, tile, LANES)
            for j in range(1, group):
                target = ahead(j)
                sel = jnp.int32(0)
                for h in range(hosts):
                    sel = jnp.where(root_ref[gz * hosts + h] == target, h, sel)
                p_out[l][c][j - 1] = replica[c][sel]
                p_copy(l, c, j).start()

        own_step = blocks_of(own_n)
        split_n = rows_n - own_n

        def with_hosted(at, n):
            return jnp.concatenate(
                [
                    acc[pl.ds(at, n), lanes(c)] + dot(dense[pl.ds(at, n), rows_n:], hosted[c][...])
                    for c in range(parts)
                ],
                axis=1,
            )

        def own(i, carry):
            at = pl.multiple_of(i * own_step, own_step)
            neighbours = with_hosted(at, own_step).astype(BF16)
            emit(
                pl.ds(at, own_step),
                dot(flat[pl.ds(at, own_step), :], w_self[...]) + dot(neighbours, w_neigh[...]),
            )
            return carry

        lax.fori_loop(0, own_n // own_step, own, 0)
        acc[own_n:rows_n, :] = with_hosted(own_n, split_n)
        selfs = dot(flat[own_n:rows_n, :], w_self[...])

        for c in range(parts):
            for j in range(1, group):
                p_copy(l, c, j).wait_recv()
            for s in range(SPLIT):
                at = own_n + s * tile
                total = acc[at : at + tile, lanes(c)]
                for j in range(1, group):
                    q = behind(j)
                    count = jnp.int32(0)
                    for h in range(hosts):
                        spot = q * hosts + h
                        count = count + jnp.where(
                            (root_ref[spot] == gz) & (block_ref[spot] == s), 1, 0
                        )
                    total = total + count.astype(F32) * p_in[l][c][j - 1].astype(F32)
                acc[at : at + tile, lanes(c)] = total
        emit(slice(own_n, rows_n), selfs + dot(acc[own_n:rows_n, :].astype(BF16), w_neigh[...]))

    def keep(at, value):
        first[at, :] = value

    layer(0, feat, lambda block, at, c: block, ws1, wn1, keep)

    value = first[...]
    sums = jnp.sum(value, axis=0, keepdims=True)
    squares = jnp.sum(value * value, axis=0, keepdims=True)
    z_out[...] = jnp.concatenate([sums, squares, jnp.zeros((6, width), F32)], axis=0)
    for j in range(1, group):
        zs_copy(j).start()
    center = sums * (1.0 / rows_n)
    delta[...] = (first[own_n:rows_n, :] - center).astype(BF16).reshape(SPLIT, tile, width)
    spread(1, delta, 0)

    total = z_out[...]
    for j in range(1, group):
        zs_copy(j).wait_recv()
        total = total + z_in[j - 1]
    xy_out[...] = total
    for n in range(len(spots)):
        xy_copy(n).start()
    for n in range(len(spots)):
        xy_copy(n).wait_recv()
        total = total + xy_in[n]
    count = rows_n * nx * ny * group
    mean = total[0:1, :] / count
    var = total[1:2, :] / count - mean * mean
    gain = lax.rsqrt(var + 1e-05) * scale_ref[...]
    shift = shift_ref[...]

    hidden[...] = (
        jnp.maximum((first[...] - mean) * gain + shift, 0.0)
        .astype(BF16)
        .reshape(rooted, tile, width)
    )

    def normal(block, at, c):
        middle = z_in[at][0:1, lanes(c)] * (1.0 / rows_n)
        moved = block.astype(F32) + (middle - mean[:, lanes(c)])
        return jnp.maximum(moved * gain[:, lanes(c)] + shift[:, lanes(c)], 0.0).astype(BF16)

    def finish(at, value):
        out_ref[at, :] = value.astype(BF16)

    layer(1, hidden, normal, ws2, wn2, finish)

    for l in range(2):
        for c in range(parts):
            for j in range(1, group):
                f_copy(l, c, j).wait_send()
                p_copy(l, c, j).wait_send()
    for j in range(1, group):
        zs_copy(j).wait_send()
    for n in range(len(spots)):
        xy_copy(n).wait_send()


def per_device(
    features,
    tile_values,
    tile_columns,
    tile_present,
    host_root,
    host_block,
    self_one,
    neigh_one,
    scale_one,
    shift_one,
    self_two,
    neigh_two,
):
    slots, ks, tile, _ = tile_values.shape
    width = features.shape[1]
    rooted = features.shape[0] // tile
    hosts = slots - rooted
    nx, ny, group = (lax.axis_size(name) for name in ("gx", "gy", "gz"))
    peers, spots = group - 1, nx * ny - 1
    parts = width // LANES
    rows_n = rooted * tile
    sizes = (nx, ny, group, slots, ks, tile, width, rooted)

    box = pltpu.VMEM((peers, tile, LANES), BF16)
    dma = pltpu.SemaphoreType.DMA
    scratch = [
        pltpu.VMEM((rooted, tile, width), BF16),
        pltpu.VMEM(tile_values.shape, BF16),
        *[pltpu.VMEM((width, width), BF16)] * 4,
        pltpu.VMEM((slots * tile, slots * tile), BF16),
        pltpu.VMEM((slots * tile, width), F32),
        pltpu.VMEM((rows_n, width), F32),
        pltpu.VMEM((rooted, tile, width), BF16),
        pltpu.VMEM((SPLIT, tile, width), BF16),
        *[pltpu.VMEM((hosts * tile, LANES), BF16)] * parts,
        *[pltpu.VMEM((hosts, tile, LANES), BF16)] * parts,
        *[box] * (8 * parts),
        pltpu.VMEM((8, width), F32),
        pltpu.VMEM((peers, 8, width), F32),
        pltpu.VMEM((8, width), F32),
        pltpu.VMEM((spots, 8, width), F32),
        dma((6,)),
        *[dma((2, parts, peers))] * 4,
        *[dma((peers,))] * 2,
        *[dma((spots,))] * 2,
    ]
    smem = pl.BlockSpec(memory_space=pltpu.SMEM)
    vmem = pl.BlockSpec(memory_space=pltpu.VMEM)
    anywhere = pl.BlockSpec(memory_space=pl.ANY)
    return pl.pallas_call(
        functools.partial(kernel, sizes),
        out_shape=jax.ShapeDtypeStruct((rows_n, width), BF16),
        in_specs=[smem] * 4 + [anywhere] * 6 + [vmem] * 2,
        out_specs=vmem,
        scratch_shapes=scratch,
        compiler_params=pltpu.CompilerParams(
            collective_id=0, has_side_effects=True, vmem_limit_bytes=40 * 1024 * 1024
        ),
    )(
        tile_columns,
        tile_present,
        host_root,
        host_block,
        features.reshape(rooted, tile, width),
        tile_values,
        self_one,
        neigh_one,
        self_two,
        neigh_two,
        scale_one.reshape(1, width),
        shift_one.reshape(1, width),
    )


def solution(mesh):
    return jax.shard_map(
        per_device,
        mesh=mesh,
        in_specs=(
            P(("gx", "gy", "gz"), None),
            P(("gx", "gy", "gz"), None, None, None),
            P(("gx", "gy", "gz"), None),
            P(("gx", "gy", "gz"), None),
            P(("gx", "gy")),
            P(("gx", "gy")),
            P(),
            P(),
            P(),
            P(),
            P(),
            P(),
        ),
        out_specs=P(("gx", "gy", "gz"), None),
        check_vma=False,
    )
```

time: 119 us -> 49 us (0.41)
  blocking collectives: 50.6 us -> 0 us
  Pallas kernels: 0 us -> 37.6 us
  waiting for transfers between devices: 17.5 us -> 0 us
  matrix products: 14.7 us -> 0 us
  starting transfers between devices: 13.1 us -> 0 us
  other arithmetic: 5.78 us -> 0 us
  local copies, waits for them, and re-layouts: 16 us -> 11 us
    psum x1 -> x0, blocking collectives: 39.9 us -> none  [per_device(): lax.psum((jnp.sum(first, axis=0), jnp.sum(first * first, axis=0)), ('gx',...]
    pallas_call x0 -> x1, Pallas kernels: none -> 37.6 us  [per_device(): pl.pallas_call(functools.partial(kernel, sizes), out_shape=jax.ShapeDtype...]
    all_to_all x3 -> x0, waiting for transfers between devices: 17.5 us -> none  [the longest x2 10.1 us: collect(): lax.all_to_all(outgoing, 'gz', split_axis=0, concat_axis=0, tiled=True)]
    dot_general x12 -> x0, matrix products: 14.7 us -> none  [the longest x2 6.28 us: aggregate(): jnp.einsum('bkij,bkjf->bif', tile_values, picked, preferred_element_type=...]
    all_to_all x3 -> x0, starting transfers between devices: 13.1 us -> none  [the longest x2 6.81 us: collect(): lax.all_to_all(outgoing, 'gz', split_axis=0, concat_axis=0, tiled=True)]
    all_to_all x1 -> x0, blocking collectives: 10.7 us -> none  [spread(): lax.all_to_all(outgoing, 'gz', split_axis=0, concat_axis=0, tiled=True)]
    unnamed x18 -> x25, local copies, waits for them, and re-layouts: 1.96 us -> 11 us
    gather x4 -> x0, local copies, waits for them, and re-layouts: 6.63 us -> none  [the longest x2 5.52 us: aggregate(): picked = view[tile_columns]]
  transfers between devices with their start and end apart: 3 -> 0, of which waited for: 3 -> 0; matrix products, arithmetic and copies ran while one was open for 5% -> 0% of each run, Pallas kernels for 0% -> 0%
where the time goes in v1:
time: 49 us; the launch traced here: 48.6 us
  Pallas kernels  37.6 us (77%)
  local copies, waits for them, and re-layouts  11 us (22%)
    pallas_call x1, Pallas kernels, per_device(): pl.pallas_call(functools.partial(kernel, sizes), out_shape=jax.ShapeDtype...  37.6 us
    unnamed x25, local copies, waits for them, and re-layouts  11 us

profile of v1, /device:TPU:0, one launch (start us, length us, event | category | flops | bytes accessed | tf_op | source)
XLA Modules:
  0.0 48.6 jit_solution(16920498408734229326)
XLA Ops:
  0.0 0.0 copy-start
  0.0 1.6 %copy-done = bf16[8,8,128,128]{3,2,1,0:T(8,128)(2,1)S(1)} copy-done((bf16[8,8,128,128]{3,2,1,0:T(8,128)(2,1)S(1)}, bf16[8,8,128,128]{3,2,1,0:T(8,128)(2,1)}, u32[]{:S(2)}) %copy-start) | copy-done | bytes 2097176
  1.6 0.0 copy-start.1
  1.6 1.0 %copy-done.1 = bf16[768,256]{1,0:T(8,128)(2,1)S(1)} copy-done((bf16[768,256]{1,0:T(8,128)(2,1)S(1)}, bf16[768,256]{1,0:T(8,128)(2,1)}, u32[]{:S(2)}) %copy-start.1) | copy-done | bytes 393240
  2.6 0.0 copy-start.2
  2.6 0.9 %copy-done.2 = bf16[256,256]{1,0:T(8,128)(2,1)S(1)} copy-done((bf16[256,256]{1,0:T(8,128)(2,1)S(1)}, bf16[256,256]{1,0:T(8,128)(2,1)}, u32[]{:S(2)}) %copy-start.2) | copy-done | bytes 131096
  3.5 0.0 copy-start.3
  3.5 0.9 %copy-done.3 = bf16[256,256]{1,0:T(8,128)(2,1)S(1)} copy-done((bf16[256,256]{1,0:T(8,128)(2,1)S(1)}, bf16[256,256]{1,0:T(8,128)(2,1)}, u32[]{:S(2)}) %copy-start.3) | copy-done | bytes 131096
  4.4 0.0 copy-start.4
  4.4 0.9 %copy-done.4 = bf16[256,256]{1,0:T(8,128)(2,1)S(1)} copy-done((bf16[256,256]{1,0:T(8,128)(2,1)S(1)}, bf16[256,256]{1,0:T(8,128)(2,1)}, u32[]{:S(2)}) %copy-start.4) | copy-done | bytes 131096
  5.3 0.0 copy-start.5
  5.3 0.9 %copy-done.5 = bf16[256,256]{1,0:T(8,128)(2,1)S(1)} copy-done((bf16[256,256]{1,0:T(8,128)(2,1)S(1)}, bf16[256,256]{1,0:T(8,128)(2,1)}, u32[]{:S(2)}) %copy-start.5) | copy-done | bytes 131096
  6.2 0.0 copy-start.6
  6.2 0.7 %copy-done.6 = s32[8,8]{1,0:T(8,128)S(1)} copy-done((s32[8,8]{1,0:T(8,128)S(1)}, s32[8,8]{1,0:T(8,128)}, u32[]{:S(2)}) %copy-start.6) | copy-done | bytes 280
  6.9 0.0 copy-start.7
  6.9 0.7 %copy-done.7 = s32[8,8]{1,0:T(8,128)S(1)} copy-done((s32[8,8]{1,0:T(8,128)S(1)}, s32[8,8]{1,0:T(8,128)}, u32[]{:S(2)}) %copy-start.7) | copy-done | bytes 280
  7.6 0.0 copy-start.8
  7.6 0.7 %copy-done.8 = f32[256]{0:T(256)S(1)} copy-done((f32[256]{0:T(256)S(1)}, f32[256]{0:T(256)}, u32[]{:S(2)}) %copy-start.8) | copy-done | bytes 1048
  8.3 0.0 copy-start.9
  8.3 0.7 %copy-done.9 = f32[256]{0:T(256)S(1)} copy-done((f32[256]{0:T(256)S(1)}, f32[256]{0:T(256)}, u32[]{:S(2)}) %copy-start.9) | copy-done | bytes 1048
  8.9 0.0 copy-start.10
  8.9 0.7 %copy-done.10 = s32[8]{0:T(128)S(1)} copy-done((s32[8]{0:T(128)S(1)}, s32[8]{0:T(128)}, u32[]{:S(2)}) %copy-start.10) | copy-done | bytes 56
  9.6 0.0 copy-start.11
  9.6 0.7 %copy-done.11 = s32[8]{0:T(128)S(1)} copy-done((s32[8]{0:T(128)S(1)}, s32[8]{0:T(128)}, u32[]{:S(2)}) %copy-start.11) | copy-done | bytes 56
  10.3 37.6 %shard_map.118 = bf16[768,256]{1,0:T(8,128)(2,1)S(1)} custom-call(s32[8,8]{1,0:T(8,128)S(1)} %copy-done.6, s32[8,8]{1,0:T(8,128)S(1)} %copy-done.7, s32[8]{0:T(128)S(1)} %copy-done.10, s32[8]{0:T(128)S(1)} %copy-done.11, bf16[6,128,256]{2,1,0:T(8,128)(2,1)S(1)} %bitcast.3, bf16[8,8,128,128]{3,2,1,0:T(8,128)(2,1)S(1)} %copy-done, ...), custom_call_target="tpu_custom_call" | custom-call | tf_op jit(solution)/shard_map/pallas_call | solution.py:348
  47.9 0.7 %copy.14 = bf16[768,256]{1,0:T(8,128)(2,1)} copy(bf16[768,256]{1,0:T(8,128)(2,1)S(1)} %shard_map.118) | data formatting | bytes 786432
Async XLA Ops:
  0.0 1.6 %copy-start = (bf16[8,8,128,128]{3,2,1,0:T(8,128)(2,1)S(1)}, bf16[8,8,128,128]{3,2,1,0:T(8,128)(2,1)}, u32[]{:S(2)}) copy-start(bf16[8,8,128,128]{3,2,1,0:T(8,128)(2,1)} %tiles_hbm.1) | copy-start | bytes 6291460
  1.6 1.0 %copy-start.1 = (bf16[768,256]{1,0:T(8,128)(2,1)S(1)}, bf16[768,256]{1,0:T(8,128)(2,1)}, u32[]{:S(2)}) copy-start(bf16[768,256]{1,0:T(8,128)(2,1)} %param.12) | copy-start | bytes 1179652
  2.6 0.9 %copy-start.2 = (bf16[256,256]{1,0:T(8,128)(2,1)S(1)}, bf16[256,256]{1,0:T(8,128)(2,1)}, u32[]{:S(2)}) copy-start(bf16[256,256]{1,0:T(8,128)(2,1)} %self_one_hbm.1) | copy-start | bytes 393220
  3.5 0.9 %copy-start.3 = (bf16[256,256]{1,0:T(8,128)(2,1)S(1)}, bf16[256,256]{1,0:T(8,128)(2,1)}, u32[]{:S(2)}) copy-start(bf16[256,256]{1,0:T(8,128)(2,1)} %neigh_one_hbm.1) | copy-start | bytes 393220
  4.4 0.9 %copy-start.4 = (bf16[256,256]{1,0:T(8,128)(2,1)S(1)}, bf16[256,256]{1,0:T(8,128)(2,1)}, u32[]{:S(2)}) copy-start(bf16[256,256]{1,0:T(8,128)(2,1)} %self_two_hbm.1) | copy-start | bytes 393220
  5.3 0.9 %copy-start.5 = (bf16[256,256]{1,0:T(8,128)(2,1)S(1)}, bf16[256,256]{1,0:T(8,128)(2,1)}, u32[]{:S(2)}) copy-start(bf16[256,256]{1,0:T(8,128)(2,1)} %neigh_two_hbm.1) | copy-start | bytes 393220
  6.2 0.7 %copy-start.6 = (s32[8,8]{1,0:T(8,128)S(1)}, s32[8,8]{1,0:T(8,128)}, u32[]{:S(2)}) copy-start(s32[8,8]{1,0:T(8,128)} %columns_ref.1) | copy-start | bytes 772
  6.9 0.7 %copy-start.7 = (s32[8,8]{1,0:T(8,128)S(1)}, s32[8,8]{1,0:T(8,128)}, u32[]{:S(2)}) copy-start(s32[8,8]{1,0:T(8,128)} %present_ref.1) | copy-start | bytes 772
  7.6 0.7 %copy-start.8 = (f32[256]{0:T(256)S(1)}, f32[256]{0:T(256)}, u32[]{:S(2)}) copy-start(f32[256]{0:T(256)} %param.20) | copy-start | bytes 3076
  8.3 0.7 %copy-start.9 = (f32[256]{0:T(256)S(1)}, f32[256]{0:T(256)}, u32[]{:S(2)}) copy-start(f32[256]{0:T(256)} %param.21) | copy-start | bytes 3076
  8.9 0.7 %copy-start.10 = (s32[8]{0:T(128)S(1)}, s32[8]{0:T(128)}, u32[]{:S(2)}) copy-start(s32[8]{0:T(128)} %root_ref.1) | copy-start | bytes 100
  9.6 0.7 %copy-start.11 = (s32[8]{0:T(128)S(1)}, s32[8]{0:T(128)}, u32[]{:S(2)}) copy-start(s32[8]{0:T(128)} %block_ref.1) | copy-start | bytes 100

commit v2 on v1

v2 whole, which is shorter than its diff:
```python
import functools

import jax
import jax.numpy as jnp
from jax import lax
from jax.experimental import pallas as pl
from jax.experimental.pallas import tpu as pltpu
from jax.sharding import PartitionSpec as P

OWN = 4
SPLIT = 2
LANES = 128
F32 = jnp.float32
BF16 = jnp.bfloat16


def dot(a, b):
    return jnp.dot(a, b, preferred_element_type=F32)


def kernel(
    sizes,
    columns_hbm,
    present_hbm,
    root_hbm,
    block_hbm,
    features_hbm,
    tiles_hbm,
    self_one_hbm,
    neigh_one_hbm,
    self_two_hbm,
    neigh_two_hbm,
    scale_hbm,
    shift_hbm,
    out_ref,
    *scratch,
):
    nx, ny, group, slots, ks, tile, width, rooted = sizes
    hosts = slots - rooted
    rows_n = rooted * tile
    own_n = OWN * tile
    parts = width // LANES
    peers = group - 1
    scratch = list(scratch)

    def take(n):
        got = scratch[:n]
        del scratch[:n]
        return got

    columns_ref, present_ref, root_ref, block_ref = take(4)
    feat, tiles, ws1, wn1, ws2, wn2, scale_ref, shift_ref = take(8)
    dense, acc, first, hidden, before = take(5)
    total_split = take(parts)
    hosted = take(parts)
    replica = take(parts)
    f_in = [take(parts) for _ in range(2)]
    f_out = [take(parts) for _ in range(2)]
    p_in = [take(parts) for _ in range(2)]
    p_out = [take(parts) for _ in range(2)]
    z_out, z_in, xy_out, xy_in = take(4)
    local_sem, f_send, f_recv, p_send, p_recv, z_send, z_recv, xy_send, xy_recv = take(9)

    gx, gy, gz = lax.axis_index("gx"), lax.axis_index("gy"), lax.axis_index("gz")
    loads = [
        pltpu.make_async_copy(src, dst, local_sem.at[i])
        for i, (src, dst) in enumerate(
            zip(
                (
                    root_hbm,
                    block_hbm,
                    features_hbm,
                    columns_hbm,
                    present_hbm,
                    tiles_hbm,
                    self_one_hbm,
                    neigh_one_hbm,
                    self_two_hbm,
                    neigh_two_hbm,
                    scale_hbm,
                    shift_hbm,
                ),
                (
                    root_ref,
                    block_ref,
                    feat,
                    columns_ref,
                    present_ref,
                    tiles,
                    ws1,
                    wn1,
                    ws2,
                    wn2,
                    scale_ref,
                    shift_ref,
                ),
            )
        )
    ]
    for load in loads:
        load.start()

    def ahead(j):
        return lax.rem(gz + j, group)

    def behind(j):
        return lax.rem(gz + group - j, group)

    spots = [(i, k) for i in range(nx) for k in range(ny) if (i, k) != (0, 0)]

    def spot_id(spot):
        return {"gx": lax.rem(gx + spot[0], nx), "gy": lax.rem(gy + spot[1], ny)}

    barrier = pltpu.get_barrier_semaphore()
    for j in range(1, group):
        pl.semaphore_signal(
            barrier, inc=1, device_id={"gz": ahead(j)}, device_id_type=pl.DeviceIdType.MESH
        )
    for spot in spots:
        pl.semaphore_signal(
            barrier, inc=1, device_id=spot_id(spot), device_id_type=pl.DeviceIdType.MESH
        )

    def z_copy(src, dst, send, recv, j):
        return pltpu.make_async_remote_copy(
            src_ref=src,
            dst_ref=dst,
            send_sem=send,
            recv_sem=recv,
            device_id={"gz": ahead(j)},
            device_id_type=pl.DeviceIdType.MESH,
        )

    def f_copy(l, c, j):
        return z_copy(
            f_out[l][c].at[j - 1], f_in[l][c].at[j - 1], f_send.at[l, c, j - 1], f_recv.at[l, c, j - 1], j
        )

    def p_copy(l, c, j):
        return z_copy(
            p_out[l][c].at[j - 1], p_in[l][c].at[j - 1], p_send.at[l, c, j - 1], p_recv.at[l, c, j - 1], j
        )

    def zs_copy(j):
        return z_copy(z_out, z_in.at[j - 1], z_send.at[j - 1], z_recv.at[j - 1], j)

    def xy_copy(n):
        return pltpu.make_async_remote_copy(
            src_ref=xy_out,
            dst_ref=xy_in.at[n],
            send_sem=xy_send.at[n],
            recv_sem=xy_recv.at[n],
            device_id=spot_id(spots[n]),
            device_id_type=pl.DeviceIdType.MESH,
        )

    def lanes(c):
        return slice(c * LANES, (c + 1) * LANES)

    def wanted(j):
        q = ahead(j)
        sel = jnp.int32(0)
        for h in range(hosts):
            at = q * hosts + h
            sel = jnp.where(root_ref[at] == gz, block_ref[at], sel)
        return sel

    def spread(l, c, block):
        for j in range(1, group):
            f_out[l][c][j - 1] = block(wanted(j))
            f_copy(l, c, j).start()

    for load in loads[:3]:
        load.wait()
    pl.semaphore_wait(barrier, peers + len(spots))
    for c in range(parts):
        spread(0, c, lambda sel: feat[OWN + sel][:, lanes(c)])

    for load in loads[3:6]:
        load.wait()

    def build(b, carry):
        at = pl.multiple_of(b * tile, tile)
        for c in range(slots):
            total = jnp.zeros((tile, tile), BF16)
            for k in range(ks):
                on = (columns_ref[b, k] == c) & (present_ref[b, k] > 0)
                total = total + jnp.where(on, tiles[b, k], jnp.zeros((tile, tile), BF16))
            dense[pl.ds(at, tile), c * tile : (c + 1) * tile] = total
        return carry

    lax.fori_loop(0, slots, build, 0)
    for load in loads[6:]:
        load.wait()

    def blocks_of(n):
        return 2 * tile if n % (2 * tile) == 0 else tile

    def local(rows, start, stop):
        step = blocks_of(stop - start)
        flat = rows.reshape(rows_n, width)

        def one(i, carry):
            at = pl.multiple_of(start + i * step, tile)
            acc[pl.ds(at, step), :] = dot(dense[pl.ds(at, step), 0:rows_n], flat[...])
            return carry

        lax.fori_loop(0, (stop - start) // step, one, 0)

    def arrived(l, c):
        for j in range(1, group):
            f_copy(l, c, j).wait_recv()

    def unpack(l, c):
        blocks = []
        for h in range(hosts):
            root = root_ref[gz * hosts + h]
            at = jnp.maximum(lax.rem(gz - root + group, group) - 1, 0)
            blocks.append(f_in[l][c][at])
        return jnp.concatenate(blocks, axis=0)

    def collect(l, c):
        part = acc[rows_n:, lanes(c)] + dot(dense[rows_n:, rows_n:], hosted[c][...])
        replica[c][...] = part.astype(BF16).reshape(hosts, tile, LANES)
        for j in range(1, group):
            target = ahead(j)
            sel = jnp.int32(0)
            for h in range(hosts):
                sel = jnp.where(root_ref[gz * hosts + h] == target, h, sel)
            p_out[l][c][j - 1] = replica[c][sel]
            p_copy(l, c, j).start()

    split_n = rows_n - own_n

    def with_hosted(at, n):
        return [
            acc[pl.ds(at, n), lanes(c)] + dot(dense[pl.ds(at, n), rows_n:], hosted[c][...])
            for c in range(parts)
        ]

    def own(rows, w_self, w_neigh, emit):
        flat = rows.reshape(rows_n, width)
        step = blocks_of(own_n)

        def one(i, carry):
            at = pl.multiple_of(i * step, step)
            neighbours = jnp.concatenate(with_hosted(at, step), axis=1).astype(BF16)
            emit(
                pl.ds(at, step),
                dot(flat[pl.ds(at, step), :], w_self[...]) + dot(neighbours, w_neigh[...]),
            )
            return carry

        lax.fori_loop(0, own_n // step, one, 0)
        for c, value in enumerate(with_hosted(own_n, split_n)):
            acc[own_n:rows_n, lanes(c)] = value
        return dot(flat[own_n:rows_n, :], w_self[...])

    def receive(l, c):
        for j in range(1, group):
            p_copy(l, c, j).wait_recv()
        for s in range(SPLIT):
            at = own_n + s * tile
            total = acc[at : at + tile, lanes(c)]
            for j in range(1, group):
                q = behind(j)
                count = jnp.int32(0)
                for h in range(hosts):
                    spot = q * hosts + h
                    count = count + jnp.where((root_ref[spot] == gz) & (block_ref[spot] == s), 1, 0)
                total = total + count.astype(F32) * p_in[l][c][j - 1].astype(F32)
            total_split[c][s] = total.astype(BF16)

    def split_neighbours():
        return jnp.concatenate(
            [total_split[c][...].reshape(split_n, LANES) for c in range(parts)], axis=1
        )

    local(feat, rows_n, slots * tile)
    local(feat, 0, rows_n)
    for c in range(parts):
        arrived(0, c)
        hosted[c][...] = unpack(0, c)
        collect(0, c)

    def keep(at, value):
        first[at, :] = value

    selfs = own(feat, ws1, wn1, keep)
    before[...] = dot(jnp.concatenate([hosted[c][...] for c in range(parts)], axis=1), ws1[...])
    value = first[0:own_n, :]
    sums = jnp.sum(value, axis=0, keepdims=True)
    squares = jnp.sum(value * value, axis=0, keepdims=True)

    for c in range(parts):
        receive(0, c)
        spread(1, c, lambda sel: total_split[c][sel])
    value = selfs + dot(split_neighbours(), wn1[...])
    first[own_n:rows_n, :] = value
    sums = sums + jnp.sum(value, axis=0, keepdims=True)
    squares = squares + jnp.sum(value * value, axis=0, keepdims=True)

    total = jnp.concatenate([sums, squares, jnp.zeros((6, width), F32)], axis=0)
    xy_out[...] = total
    for n in range(len(spots)):
        xy_copy(n).start()
    for n in range(len(spots)):
        xy_copy(n).wait_recv()
        total = total + xy_in[n]
    z_out[...] = total
    for j in range(1, group):
        zs_copy(j).start()
    for j in range(1, group):
        zs_copy(j).wait_recv()
        total = total + z_in[j - 1]
    count = rows_n * nx * ny * group
    mean = total[0:1, :] / count
    var = total[1:2, :] / count - mean * mean
    gain = lax.rsqrt(var + 1e-05) * scale_ref[...]
    shift = shift_ref[...]

    def normal(value):
        return jnp.maximum((value - mean) * gain + shift, 0.0).astype(BF16)

    hidden[...] = normal(first[...]).reshape(rooted, tile, width)
    local(hidden, rows_n, slots * tile)
    for c in range(parts):
        arrived(1, c)
    totals = jnp.concatenate([unpack(1, c) for c in range(parts)], axis=1)
    view = normal(before[...] + dot(totals, wn1[...]))
    for c in range(parts):
        hosted[c][...] = view[:, lanes(c)]
        collect(1, c)

    def finish(at, value):
        out_ref[at, :] = value.astype(BF16)

    local(hidden, 0, rows_n)
    selfs = own(hidden, ws2, wn2, finish)
    for c in range(parts):
        receive(1, c)
    finish(slice(own_n, rows_n), selfs + dot(split_neighbours(), wn2[...]))

    for l in range(2):
        for c in range(parts):
            for j in range(1, group):
                f_copy(l, c, j).wait_send()
                p_copy(l, c, j).wait_send()
    for j in range(1, group):
        zs_copy(j).wait_send()
    for n in range(len(spots)):
        xy_copy(n).wait_send()


def per_device(
    features,
    tile_values,
    tile_columns,
    tile_present,
    host_root,
    host_block,
    self_one,
    neigh_one,
    scale_one,
    shift_one,
    self_two,
    neigh_two,
):
    slots, ks, tile, _ = tile_values.shape
    width = features.shape[1]
    rooted = features.shape[0] // tile
    hosts = slots - rooted
    nx, ny, group = (lax.axis_size(name) for name in ("gx", "gy", "gz"))
    peers, spots = group - 1, nx * ny - 1
    parts = width // LANES
    rows_n = rooted * tile
    sizes = (nx, ny, group, slots, ks, tile, width, rooted)

    box = pltpu.VMEM((peers, tile, LANES), BF16)
    dma = pltpu.SemaphoreType.DMA
    scratch = [
        *[pltpu.SMEM(tile_columns.shape, jnp.int32)] * 2,
        *[pltpu.SMEM(host_root.shape, jnp.int32)] * 2,
        pltpu.VMEM((rooted, tile, width), BF16),
        pltpu.VMEM(tile_values.shape, BF16),
        *[pltpu.VMEM((width, width), BF16)] * 4,
        *[pltpu.VMEM((1, width), F32)] * 2,
        pltpu.VMEM((slots * tile, slots * tile), BF16),
        pltpu.VMEM((slots * tile, width), F32),
        pltpu.VMEM((rows_n, width), F32),
        pltpu.VMEM((rooted, tile, width), BF16),
        pltpu.VMEM((hosts * tile, width), F32),
        *[pltpu.VMEM((SPLIT, tile, LANES), BF16)] * parts,
        *[pltpu.VMEM((hosts * tile, LANES), BF16)] * parts,
        *[pltpu.VMEM((hosts, tile, LANES), BF16)] * parts,
        *[box] * (8 * parts),
        pltpu.VMEM((8, width), F32),
        pltpu.VMEM((peers, 8, width), F32),
        pltpu.VMEM((8, width), F32),
        pltpu.VMEM((spots, 8, width), F32),
        dma((12,)),
        *[dma((2, parts, peers))] * 4,
        *[dma((peers,))] * 2,
        *[dma((spots,))] * 2,
    ]
    vmem = pl.BlockSpec(memory_space=pltpu.VMEM)
    hbm = pl.BlockSpec(memory_space=pltpu.HBM)
    call = pl.pallas_call(
        functools.partial(kernel, sizes),
        out_shape=jax.ShapeDtypeStruct((rows_n, width), BF16),
        in_specs=[hbm] * 12,
        out_specs=vmem,
        scratch_shapes=scratch,
        compiler_params=pltpu.CompilerParams(
            collective_id=0, has_side_effects=True, vmem_limit_bytes=40 * 1024 * 1024
        ),
    )
    operands = (
        tile_columns,
        tile_present,
        host_root,
        host_block,
        features.reshape(rooted, tile, width),
        tile_values,
        self_one,
        neigh_one,
        self_two,
        neigh_two,
        scale_one.reshape(1, width),
        shift_one.reshape(1, width),
    )
    return call(*(pltpu.with_memory_space_constraint(x, pltpu.HBM) for x in operands))


def solution(mesh):
    return jax.shard_map(
        per_device,
        mesh=mesh,
        in_specs=(
            P(("gx", "gy", "gz"), None),
            P(("gx", "gy", "gz"), None, None, None),
            P(("gx", "gy", "gz"), None),
            P(("gx", "gy", "gz"), None),
            P(("gx", "gy")),
            P(("gx", "gy")),
            P(),
            P(),
            P(),
            P(),
            P(),
            P(),
        ),
        out_specs=P(("gx", "gy", "gz"), None),
        check_vma=False,
    )
```

time: 49 us -> 37.5 us (0.77)
  local copies, waits for them, and re-layouts: 11 us -> 0.75 us
  Pallas kernels: 37.6 us -> 36.6 us
    unnamed x25 -> x1, local copies, waits for them, and re-layouts: 11 us -> 0.75 us
    pallas_call x1, Pallas kernels: 37.6 us -> 36.6 us  [per_device(): call(*(pltpu.with_memory_space_constraint(x, pltpu.HBM) for x in operands))]
where the time goes in v2:
time: 37.5 us; the launch traced here: 37.4 us
  Pallas kernels  36.6 us (98%)
  local copies, waits for them, and re-layouts  0.75 us (2%)
    pallas_call x1, Pallas kernels, per_device(): call(*(pltpu.with_memory_space_constraint(x, pltpu.HBM) for x in operands))  36.6 us

profile of v2, /device:TPU:0, one launch (start us, length us, event | category | flops | bytes accessed | tf_op | source)
XLA Modules:
  0.0 37.4 jit_solution(17080221345393669307)
XLA Ops:
  0.0 36.6 %shard_map.118 = bf16[768,256]{1,0:T(8,128)(2,1)S(1)} custom-call(s32[8,8]{1,0:T(8,128)} %columns_hbm.1, s32[8,8]{1,0:T(8,128)} %present_hbm.1, s32[8]{0:T(128)} %root_hbm.1, s32[8]{0:T(128)} %block_hbm.1, bf16[6,128,256]{2,1,0:T(8,128)(2,1)} %bitcast.3, bf16[8,8,128,128]{3,2,1,0:T(8,128)(2,1)} %tiles_hbm.1, bf16[256,256]{1,0:T(8,128)(2,1)} %self_one_hbm.1, ...), custom_call_target="tpu_custom_call" | custom-call | tf_op jit(solution)/shard_map/pallas_call | solution.py:432
  36.6 0.7 %copy.14 = bf16[768,256]{1,0:T(8,128)(2,1)} copy(bf16[768,256]{1,0:T(8,128)(2,1)S(1)} %shard_map.118) | data formatting | bytes 786432

commit v3 on v2

--- a/solution.py
+++ b/solution.py
@@ -62,43 +62,25 @@
     local_sem, f_send, f_recv, p_send, p_recv, z_send, z_recv, xy_send, xy_recv = take(9)
 
     gx, gy, gz = lax.axis_index("gx"), lax.axis_index("gy"), lax.axis_index("gz")
+    sources = (
+        (root_hbm, root_ref),
+        (block_hbm, block_ref),
+        (features_hbm.at[OWN:], feat.at[OWN:]),
+        (columns_hbm, columns_ref),
+        (present_hbm, present_ref),
+        (features_hbm.at[:OWN], feat.at[:OWN]),
+        (tiles_hbm.at[OWN:], tiles.at[OWN:]),
+        (tiles_hbm.at[:OWN], tiles.at[:OWN]),
+        (self_one_hbm, ws1),
+        (neigh_one_hbm, wn1),
+        (self_two_hbm, ws2),
+        (neigh_two_hbm, wn2),
+        (scale_hbm, scale_ref),
+        (shift_hbm, shift_ref),
+    )
     loads = [
-        pltpu.make_async_copy(src, dst, local_sem.at[i])
-        for i, (src, dst) in enumerate(
-            zip(
-                (
-                    root_hbm,
-                    block_hbm,
-                    features_hbm,
-                    columns_hbm,
-                    present_hbm,
-                    tiles_hbm,
-                    self_one_hbm,
-                    neigh_one_hbm,
-                    self_two_hbm,
-                    neigh_two_hbm,
-                    scale_hbm,
-                    shift_hbm,
-                ),
-                (
-                    root_ref,
-                    block_ref,
-                    feat,
-                    columns_ref,
-                    present_ref,
-                    tiles,
-                    ws1,
-                    wn1,
-                    ws2,
-                    wn2,
-                    scale_ref,
-                    shift_ref,
-                ),
-            )
-        )
+        pltpu.make_async_copy(src, dst, local_sem.at[i]) for i, (src, dst) in enumerate(sources)
     ]
-    for load in loads:
-        load.start()
 
     def ahead(j):
         return lax.rem(gz + j, group)
@@ -120,6 +102,9 @@
         pl.semaphore_signal(
             barrier, inc=1, device_id=spot_id(spot), device_id_type=pl.DeviceIdType.MESH
         )
+
+    for load in loads:
+        load.start()
 
     def z_copy(src, dst, send, recv, j):
         return pltpu.make_async_remote_copy(
@@ -170,13 +155,19 @@
             f_out[l][c][j - 1] = block(wanted(j))
             f_copy(l, c, j).start()
 
+    def split_feature(sel, c):
+        block = feat[OWN, :, lanes(c)]
+        for s in range(1, SPLIT):
+            block = jnp.where(sel == s, feat[OWN + s, :, lanes(c)], block)
+        return block
+
     for load in loads[:3]:
         load.wait()
     pl.semaphore_wait(barrier, peers + len(spots))
     for c in range(parts):
-        spread(0, c, lambda sel: feat[OWN + sel][:, lanes(c)])
-
-    for load in loads[3:6]:
+        spread(0, c, lambda sel: split_feature(sel, c))
+
+    for load in loads[3:7]:
         load.wait()
 
     def build(b, carry):
@@ -188,10 +179,6 @@
                 total = total + jnp.where(on, tiles[b, k], jnp.zeros((tile, tile), BF16))
             dense[pl.ds(at, tile), c * tile : (c + 1) * tile] = total
         return carry
-
-    lax.fori_loop(0, slots, build, 0)
-    for load in loads[6:]:
-        load.wait()
 
     def blocks_of(n):
         return 2 * tile if n % (2 * tile) == 0 else tile
@@ -238,12 +225,16 @@
             for c in range(parts)
         ]
 
-    def own(rows, w_self, w_neigh, emit):
+    def split_hosted():
+        for c, value in enumerate(with_hosted(own_n, split_n)):
+            acc[own_n:rows_n, lanes(c)] = value
+
+    def own(rows, w_self, w_neigh, start, stop, emit):
         flat = rows.reshape(rows_n, width)
-        step = blocks_of(own_n)
+        step = blocks_of(stop - start)
 
         def one(i, carry):
-            at = pl.multiple_of(i * step, step)
+            at = pl.multiple_of(start + i * step, tile)
             neighbours = jnp.concatenate(with_hosted(at, step), axis=1).astype(BF16)
             emit(
                 pl.ds(at, step),
@@ -251,10 +242,13 @@
             )
             return carry
 
-        lax.fori_loop(0, own_n // step, one, 0)
-        for c, value in enumerate(with_hosted(own_n, split_n)):
-            acc[own_n:rows_n, lanes(c)] = value
-        return dot(flat[own_n:rows_n, :], w_self[...])
+        lax.fori_loop(0, (stop - start) // step, one, 0)
+
+    def split_self(rows, w_self):
+        return dot(rows.reshape(rows_n, width)[own_n:rows_n, :], w_self[...])
+
+    def split_neigh(c, w_neigh):
+        return dot(total_split[c][...].reshape(split_n, LANES), w_neigh[lanes(c), :])
 
     def receive(l, c):
         for j in range(1, group):
@@ -271,48 +265,58 @@
                 total = total + count.astype(F32) * p_in[l][c][j - 1].astype(F32)
             total_split[c][s] = total.astype(BF16)
 
-    def split_neighbours():
-        return jnp.concatenate(
-            [total_split[c][...].reshape(split_n, LANES) for c in range(parts)], axis=1
-        )
-
+    lax.fori_loop(rooted, slots, build, 0)
     local(feat, rows_n, slots * tile)
-    local(feat, 0, rows_n)
+    lax.fori_loop(OWN, rooted, build, 0)
+    local(feat, own_n, rows_n)
     for c in range(parts):
         arrived(0, c)
         hosted[c][...] = unpack(0, c)
         collect(0, c)
+    split_hosted()
+    for load in loads[7:]:
+        load.wait()
 
     def keep(at, value):
         first[at, :] = value
 
-    selfs = own(feat, ws1, wn1, keep)
-    before[...] = dot(jnp.concatenate([hosted[c][...] for c in range(parts)], axis=1), ws1[...])
-    value = first[0:own_n, :]
-    sums = jnp.sum(value, axis=0, keepdims=True)
-    squares = jnp.sum(value * value, axis=0, keepdims=True)
-
+    edges = [own_n * i // parts // tile * tile for i in range(parts + 1)]
+    value = split_self(feat, ws1)
     for c in range(parts):
+        start, stop = edges[c], edges[c + 1]
+        lax.fori_loop(start // tile, stop // tile, build, 0)
+        local(feat, start, stop)
+        own(feat, ws1, wn1, start, stop, keep)
+        if c == parts - 1:
+            mine = first[0:own_n, :]
+            sums = jnp.sum(mine, axis=0, keepdims=True)
+            squares = jnp.sum(mine * mine, axis=0, keepdims=True)
         receive(0, c)
-        spread(1, c, lambda sel: total_split[c][sel])
-    value = selfs + dot(split_neighbours(), wn1[...])
+        if c < parts - 1:
+            spread(1, c, lambda sel: total_split[c][sel])
+        value = value + split_neigh(c, wn1)
     first[own_n:rows_n, :] = value
     sums = sums + jnp.sum(value, axis=0, keepdims=True)
     squares = squares + jnp.sum(value * value, axis=0, keepdims=True)
 
     total = jnp.concatenate([sums, squares, jnp.zeros((6, width), F32)], axis=0)
+    z_out[...] = total
+    for j in range(1, group):
+        zs_copy(j).start()
+    spread(1, parts - 1, lambda sel: total_split[parts - 1][sel])
+    before[...] = dot(jnp.concatenate([hosted[c][...] for c in range(parts)], axis=1), ws1[...])
+    for j in range(1, group):
+        zs_copy(j).wait_recv()
+        total = total + z_in[j - 1]
     xy_out[...] = total
     for n in range(len(spots)):
         xy_copy(n).start()
+    for c in range(parts - 1):
+        arrived(1, c)
+        before[...] += dot(unpack(1, c), wn1[lanes(c), :])
     for n in range(len(spots)):
         xy_copy(n).wait_recv()
         total = total + xy_in[n]
-    z_out[...] = total
-    for j in range(1, group):
-        zs_copy(j).start()
-    for j in range(1, group):
-        zs_copy(j).wait_recv()
-        total = total + z_in[j - 1]
     count = rows_n * nx * ny * group
     mean = total[0:1, :] / count
     var = total[1:2, :] / count - mean * mean
@@ -324,10 +328,8 @@
 
     hidden[...] = normal(first[...]).reshape(rooted, tile, width)
     local(hidden, rows_n, slots * tile)
-    for c in range(parts):
-        arrived(1, c)
-    totals = jnp.concatenate([unpack(1, c) for c in range(parts)], axis=1)
-    view = normal(before[...] + dot(totals, wn1[...]))
+    arrived(1, parts - 1)
+    view = normal(before[...] + dot(unpack(1, parts - 1), wn1[lanes(parts - 1), :]))
     for c in range(parts):
         hosted[c][...] = view[:, lanes(c)]
         collect(1, c)
@@ -335,11 +337,15 @@
     def finish(at, value):
         out_ref[at, :] = value.astype(BF16)
 
-    local(hidden, 0, rows_n)
-    selfs = own(hidden, ws2, wn2, finish)
+    local(hidden, own_n, rows_n)
+    split_hosted()
+    value = split_self(hidden, ws2)
+    local(hidden, 0, own_n)
+    own(hidden, ws2, wn2, 0, own_n, finish)
     for c in range(parts):
         receive(1, c)
-    finish(slice(own_n, rows_n), selfs + dot(split_neighbours(), wn2[...]))
+        value = value + split_neigh(c, wn2)
+    finish(slice(own_n, rows_n), value)
 
     for l in range(2):
         for c in range(parts):
@@ -398,7 +404,7 @@
         pltpu.VMEM((peers, 8, width), F32),
         pltpu.VMEM((8, width), F32),
         pltpu.VMEM((spots, 8, width), F32),
-        dma((12,)),
+        dma((14,)),
         *[dma((2, parts, peers))] * 4,
         *[dma((peers,))] * 2,
         *[dma((spots,))] * 2,

time: 37.5 us -> 38.1 us (1.016)
  Pallas kernels: 36.6 us -> 37.2 us
    pallas_call x1, Pallas kernels: 36.6 us -> 37.2 us  [per_device(): call(*(pltpu.with_memory_space_constraint(x, pltpu.HBM) for x in operands))]
where the time goes in v3:
time: 38.1 us; the launch traced here: 38 us
  Pallas kernels  37.2 us (98%)
  local copies, waits for them, and re-layouts  0.75 us (2%)
    pallas_call x1, Pallas kernels, per_device(): call(*(pltpu.with_memory_space_constraint(x, pltpu.HBM) for x in operands))  37.2 us

profile of v3, /device:TPU:0, one launch (start us, length us, event | category | flops | bytes accessed | tf_op | source)
XLA Modules:
  0.0 38.0 jit_solution(9098288318907599070)
XLA Ops:
  0.0 37.2 %shard_map.118 = bf16[768,256]{1,0:T(8,128)(2,1)S(1)} custom-call(s32[8,8]{1,0:T(8,128)} %columns_hbm.1, s32[8,8]{1,0:T(8,128)} %present_hbm.1, s32[8]{0:T(128)} %root_hbm.1, s32[8]{0:T(128)} %block_hbm.1, bf16[6,128,256]{2,1,0:T(8,128)(2,1)} %bitcast.3, bf16[8,8,128,128]{3,2,1,0:T(8,128)(2,1)} %tiles_hbm.1, bf16[256,256]{1,0:T(8,128)(2,1)} %self_one_hbm.1, ...), custom_call_target="tpu_custom_call" | custom-call | tf_op jit(solution)/shard_map/pallas_call | solution.py:438
  37.2 0.7 %copy.14 = bf16[768,256]{1,0:T(8,128)(2,1)} copy(bf16[768,256]{1,0:T(8,128)(2,1)S(1)} %shard_map.118) | data formatting | bytes 786432

commit v4 on v3

--- a/solution.py
+++ b/solution.py
@@ -68,9 +68,8 @@
         (features_hbm.at[OWN:], feat.at[OWN:]),
         (columns_hbm, columns_ref),
         (present_hbm, present_ref),
+        (tiles_hbm, tiles),
         (features_hbm.at[:OWN], feat.at[:OWN]),
-        (tiles_hbm.at[OWN:], tiles.at[OWN:]),
-        (tiles_hbm.at[:OWN], tiles.at[:OWN]),
         (self_one_hbm, ws1),
         (neigh_one_hbm, wn1),
         (self_two_hbm, ws2),
@@ -150,8 +149,12 @@
             sel = jnp.where(root_ref[at] == gz, block_ref[at], sel)
         return sel
 
-    def spread(l, c, block):
-        for j in range(1, group):
+    def order(k):
+        return jnp.where(2 * gz < group, group - k, k)
+
+    def spread(l, c, block, start=1, stop=group):
+        for k in range(start, stop):
+            j = order(k)
             f_out[l][c][j - 1] = block(wanted(j))
             f_copy(l, c, j).start()
 
@@ -167,7 +170,7 @@
     for c in range(parts):
         spread(0, c, lambda sel: split_feature(sel, c))
 
-    for load in loads[3:7]:
+    for load in loads[3:6]:
         load.wait()
 
     def build(b, carry):
@@ -180,6 +183,10 @@
             dense[pl.ds(at, tile), c * tile : (c + 1) * tile] = total
         return carry
 
+    lax.fori_loop(0, slots, build, 0)
+    for load in loads[6:]:
+        load.wait()
+
     def blocks_of(n):
         return 2 * tile if n % (2 * tile) == 0 else tile
 
@@ -209,7 +216,8 @@
     def collect(l, c):
         part = acc[rows_n:, lanes(c)] + dot(dense[rows_n:, rows_n:], hosted[c][...])
         replica[c][...] = part.astype(BF16).reshape(hosts, tile, LANES)
-        for j in range(1, group):
+        for k in range(1, group):
+            j = order(k)
             target = ahead(j)
             sel = jnp.int32(0)
             for h in range(hosts):
@@ -225,16 +233,12 @@
             for c in range(parts)
         ]
 
-    def split_hosted():
-        for c, value in enumerate(with_hosted(own_n, split_n)):
-            acc[own_n:rows_n, lanes(c)] = value
-
-    def own(rows, w_self, w_neigh, start, stop, emit):
+    def own(rows, w_self, w_neigh, emit):
         flat = rows.reshape(rows_n, width)
-        step = blocks_of(stop - start)
+        step = blocks_of(own_n)
 
         def one(i, carry):
-            at = pl.multiple_of(start + i * step, tile)
+            at = pl.multiple_of(i * step, step)
             neighbours = jnp.concatenate(with_hosted(at, step), axis=1).astype(BF16)
             emit(
                 pl.ds(at, step),
@@ -242,13 +246,10 @@
             )
             return carry
 
-        lax.fori_loop(0, (stop - start) // step, one, 0)
-
-    def split_self(rows, w_self):
-        return dot(rows.reshape(rows_n, width)[own_n:rows_n, :], w_self[...])
-
-    def split_neigh(c, w_neigh):
-        return dot(total_split[c][...].reshape(split_n, LANES), w_neigh[lanes(c), :])
+        lax.fori_loop(0, own_n // step, one, 0)
+        for c, value in enumerate(with_hosted(own_n, split_n)):
+            acc[own_n:rows_n, lanes(c)] = value
+        return dot(flat[own_n:rows_n, :], w_self[...])
 
     def receive(l, c):
         for j in range(1, group):
@@ -265,36 +266,34 @@
                 total = total + count.astype(F32) * p_in[l][c][j - 1].astype(F32)
             total_split[c][s] = total.astype(BF16)
 
-    lax.fori_loop(rooted, slots, build, 0)
+    def split_neigh(c, w_neigh):
+        return dot(total_split[c][...].reshape(split_n, LANES), w_neigh[lanes(c), :])
+
     local(feat, rows_n, slots * tile)
-    lax.fori_loop(OWN, rooted, build, 0)
-    local(feat, own_n, rows_n)
+    local(feat, 0, rows_n)
     for c in range(parts):
         arrived(0, c)
         hosted[c][...] = unpack(0, c)
         collect(0, c)
-    split_hosted()
-    for load in loads[7:]:
-        load.wait()
 
     def keep(at, value):
         first[at, :] = value
 
-    edges = [own_n * i // parts // tile * tile for i in range(parts + 1)]
-    value = split_self(feat, ws1)
+    value = own(feat, ws1, wn1, keep)
+    before[...] = dot(jnp.concatenate([hosted[c][...] for c in range(parts)], axis=1), ws1[...])
+    mine = first[0:own_n, :]
+    sums = jnp.sum(mine, axis=0, keepdims=True)
+    squares = jnp.sum(mine * mine, axis=0, keepdims=True)
+
+    def totals_of(c):
+        return lambda sel: total_split[c][sel]
+
+    ahead_of_sums = 1 + peers // 3
     for c in range(parts):
-        start, stop = edges[c], edges[c + 1]
-        lax.fori_loop(start // tile, stop // tile, build, 0)
-        local(feat, start, stop)
-        own(feat, ws1, wn1, start, stop, keep)
-        if c == parts - 1:
-            mine = first[0:own_n, :]
-            sums = jnp.sum(mine, axis=0, keepdims=True)
-            squares = jnp.sum(mine * mine, axis=0, keepdims=True)
         receive(0, c)
-        if c < parts - 1:
-            spread(1, c, lambda sel: total_split[c][sel])
         value = value + split_neigh(c, wn1)
+        if c == 0:
+            spread(1, c, totals_of(c), 1, ahead_of_sums)
     first[own_n:rows_n, :] = value
     sums = sums + jnp.sum(value, axis=0, keepdims=True)
     squares = squares + jnp.sum(value * value, axis=0, keepdims=True)
@@ -303,17 +302,15 @@
     z_out[...] = total
     for j in range(1, group):
         zs_copy(j).start()
-    spread(1, parts - 1, lambda sel: total_split[parts - 1][sel])
-    before[...] = dot(jnp.concatenate([hosted[c][...] for c in range(parts)], axis=1), ws1[...])
+    spread(1, 0, totals_of(0), ahead_of_sums, group)
+    for c in range(1, parts):
+        spread(1, c, totals_of(c))
     for j in range(1, group):
         zs_copy(j).wait_recv()
         total = total + z_in[j - 1]
     xy_out[...] = total
     for n in range(len(spots)):
         xy_copy(n).start()
-    for c in range(parts - 1):
-        arrived(1, c)
-        before[...] += dot(unpack(1, c), wn1[lanes(c), :])
     for n in range(len(spots)):
         xy_copy(n).wait_recv()
         total = total + xy_in[n]
@@ -328,6 +325,9 @@
 
     hidden[...] = normal(first[...]).reshape(rooted, tile, width)
     local(hidden, rows_n, slots * tile)
+    for c in range(parts - 1):
+        arrived(1, c)
+        before[...] += dot(unpack(1, c), wn1[lanes(c), :])
     arrived(1, parts - 1)
     view = normal(before[...] + dot(unpack(1, parts - 1), wn1[lanes(parts - 1), :]))
     for c in range(parts):
@@ -337,11 +337,8 @@
     def finish(at, value):
         out_ref[at, :] = value.astype(BF16)
 
-    local(hidden, own_n, rows_n)
-    split_hosted()
-    value = split_self(hidden, ws2)
-    local(hidden, 0, own_n)
-    own(hidden, ws2, wn2, 0, own_n, finish)
+    local(hidden, 0, rows_n)
+    value = own(hidden, ws2, wn2, finish)
     for c in range(parts):
         receive(1, c)
         value = value + split_neigh(c, wn2)
@@ -404,7 +401,7 @@
         pltpu.VMEM((peers, 8, width), F32),
         pltpu.VMEM((8, width), F32),
         pltpu.VMEM((spots, 8, width), F32),
-        dma((14,)),
+        dma((13,)),
         *[dma((2, parts, peers))] * 4,
         *[dma((peers,))] * 2,
         *[dma((spots,))] * 2,

time: 38.1 us -> 37.7 us (0.990)
  Pallas kernels: 37.2 us -> 36.8 us
    pallas_call x1, Pallas kernels: 37.2 us -> 36.8 us  [per_device(): call(*(pltpu.with_memory_space_constraint(x, pltpu.HBM) for x in operands))]
where the time goes in v4:
time: 37.7 us; the launch traced here: 37.5 us
  Pallas kernels  36.8 us (98%)
  local copies, waits for them, and re-layouts  0.75 us (2%)
    pallas_call x1, Pallas kernels, per_device(): call(*(pltpu.with_memory_space_constraint(x, pltpu.HBM) for x in operands))  36.8 us

profile of v4, /device:TPU:0, one launch (start us, length us, event | category | flops | bytes accessed | tf_op | source)
XLA Modules:
  0.0 37.5 jit_solution(3801184496111421396)
XLA Ops:
  0.0 36.8 %shard_map.118 = bf16[768,256]{1,0:T(8,128)(2,1)S(1)} custom-call(s32[8,8]{1,0:T(8,128)} %columns_hbm.1, s32[8,8]{1,0:T(8,128)} %present_hbm.1, s32[8]{0:T(128)} %root_hbm.1, s32[8]{0:T(128)} %block_hbm.1, bf16[6,128,256]{2,1,0:T(8,128)(2,1)} %bitcast.3, bf16[8,8,128,128]{3,2,1,0:T(8,128)(2,1)} %tiles_hbm.1, bf16[256,256]{1,0:T(8,128)(2,1)} %self_one_hbm.1, ...), custom_call_target="tpu_custom_call" | custom-call | tf_op jit(solution)/shard_map/pallas_call | solution.py:435
  36.8 0.7 %copy.14 = bf16[768,256]{1,0:T(8,128)(2,1)} copy(bf16[768,256]{1,0:T(8,128)(2,1)S(1)} %shard_map.118) | data formatting | bytes 786432

commit v5 on v4

--- a/solution.py
+++ b/solution.py
@@ -81,16 +81,19 @@
         pltpu.make_async_copy(src, dst, local_sem.at[i]) for i, (src, dst) in enumerate(sources)
     ]
 
+    def wrap(value, size):
+        return jnp.where(value >= size, value - size, value)
+
     def ahead(j):
-        return lax.rem(gz + j, group)
+        return wrap(gz + j, group)
 
     def behind(j):
-        return lax.rem(gz + group - j, group)
+        return wrap(gz + group - j, group)
 
     spots = [(i, k) for i in range(nx) for k in range(ny) if (i, k) != (0, 0)]
 
     def spot_id(spot):
-        return {"gx": lax.rem(gx + spot[0], nx), "gy": lax.rem(gy + spot[1], ny)}
+        return {"gx": wrap(gx + spot[0], nx), "gy": wrap(gy + spot[1], ny)}
 
     barrier = pltpu.get_barrier_semaphore()
     for j in range(1, group):
@@ -149,13 +152,9 @@
             sel = jnp.where(root_ref[at] == gz, block_ref[at], sel)
         return sel
 
-    def order(k):
-        return jnp.where(2 * gz < group, group - k, k)
-
-    def spread(l, c, block, start=1, stop=group):
-        for k in range(start, stop):
-            j = order(k)
-            f_out[l][c][j - 1] = block(wanted(j))
+    def spread(l, c, block):
+        for j in range(1, group):
+            f_out[l][c][j - 1] = block(wants[j])
             f_copy(l, c, j).start()
 
     def split_feature(sel, c):
@@ -164,8 +163,29 @@
             block = jnp.where(sel == s, feat[OWN + s, :, lanes(c)], block)
         return block
 
-    for load in loads[:3]:
+    for load in loads[:2]:
         load.wait()
+    wants = {j: wanted(j) for j in range(1, group)}
+    my_roots = [root_ref[gz * hosts + h] for h in range(hosts)]
+    from_at = []
+    for root in my_roots:
+        at = wrap(gz - root + group, group) - 1
+        from_at.append(jnp.clip(at, 0, peers - 1))
+    to_sel = {}
+    holds = {}
+    for j in range(1, group):
+        target, q = ahead(j), behind(j)
+        sel = jnp.int32(0)
+        for h in range(hosts):
+            sel = jnp.where(my_roots[h] == target, h, sel)
+        to_sel[j] = sel
+        for s in range(SPLIT):
+            count = jnp.int32(0)
+            for h in range(hosts):
+                spot = q * hosts + h
+                count = count + jnp.where((root_ref[spot] == gz) & (block_ref[spot] == s), 1, 0)
+            holds[j, s] = count.astype(F32)
+    loads[2].wait()
     pl.semaphore_wait(barrier, peers + len(spots))
     for c in range(parts):
         spread(0, c, lambda sel: split_feature(sel, c))
@@ -206,23 +226,14 @@
             f_copy(l, c, j).wait_recv()
 
     def unpack(l, c):
-        blocks = []
-        for h in range(hosts):
-            root = root_ref[gz * hosts + h]
-            at = jnp.maximum(lax.rem(gz - root + group, group) - 1, 0)
-            blocks.append(f_in[l][c][at])
+        blocks = [f_in[l][c][at] for at in from_at]
         return jnp.concatenate(blocks, axis=0)
 
     def collect(l, c):
         part = acc[rows_n:, lanes(c)] + dot(dense[rows_n:, rows_n:], hosted[c][...])
         replica[c][...] = part.astype(BF16).reshape(hosts, tile, LANES)
-        for k in range(1, group):
-            j = order(k)
-            target = ahead(j)
-            sel = jnp.int32(0)
-            for h in range(hosts):
-                sel = jnp.where(root_ref[gz * hosts + h] == target, h, sel)
-            p_out[l][c][j - 1] = replica[c][sel]
+        for j in range(1, group):
+            p_out[l][c][j - 1] = replica[c][to_sel[j]]
             p_copy(l, c, j).start()
 
     split_n = rows_n - own_n
@@ -258,12 +269,7 @@
             at = own_n + s * tile
             total = acc[at : at + tile, lanes(c)]
             for j in range(1, group):
-                q = behind(j)
-                count = jnp.int32(0)
-                for h in range(hosts):
-                    spot = q * hosts + h
-                    count = count + jnp.where((root_ref[spot] == gz) & (block_ref[spot] == s), 1, 0)
-                total = total + count.astype(F32) * p_in[l][c][j - 1].astype(F32)
+                total = total + holds[j, s] * p_in[l][c][j - 1].astype(F32)
             total_split[c][s] = total.astype(BF16)
 
     def split_neigh(c, w_neigh):
@@ -288,32 +294,27 @@
     def totals_of(c):
         return lambda sel: total_split[c][sel]
 
-    ahead_of_sums = 1 + peers // 3
     for c in range(parts):
         receive(0, c)
+        spread(1, c, totals_of(c))
         value = value + split_neigh(c, wn1)
-        if c == 0:
-            spread(1, c, totals_of(c), 1, ahead_of_sums)
     first[own_n:rows_n, :] = value
     sums = sums + jnp.sum(value, axis=0, keepdims=True)
     squares = squares + jnp.sum(value * value, axis=0, keepdims=True)
 
     total = jnp.concatenate([sums, squares, jnp.zeros((6, width), F32)], axis=0)
-    z_out[...] = total
-    for j in range(1, group):
-        zs_copy(j).start()
-    spread(1, 0, totals_of(0), ahead_of_sums, group)
-    for c in range(1, parts):
-        spread(1, c, totals_of(c))
-    for j in range(1, group):
-        zs_copy(j).wait_recv()
-        total = total + z_in[j - 1]
     xy_out[...] = total
     for n in range(len(spots)):
         xy_copy(n).start()
     for n in range(len(spots)):
         xy_copy(n).wait_recv()
         total = total + xy_in[n]
+    z_out[...] = total
+    for j in range(1, group):
+        zs_copy(j).start()
+    for j in range(1, group):
+        zs_copy(j).wait_recv()
+        total = total + z_in[j - 1]
     count = rows_n * nx * ny * group
     mean = total[0:1, :] / count
     var = total[1:2, :] / count - mean * mean

time: 37.7 us -> 37.4 us (level)
  no operation moved by 1% of the time
where the time goes in v5:
time: 37.4 us; the launch traced here: 37.3 us
  Pallas kernels  36.5 us (98%)
  local copies, waits for them, and re-layouts  0.75 us (2%)
    pallas_call x1, Pallas kernels, per_device(): call(*(pltpu.with_memory_space_constraint(x, pltpu.HBM) for x in operands))  36.5 us
    unnamed x1, local copies, waits for them, and re-layouts  0.75 us

profile of v5, /device:TPU:0, one launch (start us, length us, event | category | flops | bytes accessed | tf_op | source)
XLA Modules:
  0.0 37.3 jit_solution(11337902859984624914)
XLA Ops:
  0.0 36.5 %shard_map.118 = bf16[768,256]{1,0:T(8,128)(2,1)S(1)} custom-call(s32[8,8]{1,0:T(8,128)} %columns_hbm.1, s32[8,8]{1,0:T(8,128)} %present_hbm.1, s32[8]{0:T(128)} %root_hbm.1, s32[8]{0:T(128)} %block_hbm.1, bf16[6,128,256]{2,1,0:T(8,128)(2,1)} %bitcast.3, bf16[8,8,128,128]{3,2,1,0:T(8,128)(2,1)} %tiles_hbm.1, bf16[256,256]{1,0:T(8,128)(2,1)} %self_one_hbm.1, ...), custom_call_target="tpu_custom_call" | custom-call | tf_op jit(solution)/shard_map/pallas_call | solution.py:436
  36.5 0.7 %copy.14 = bf16[768,256]{1,0:T(8,128)(2,1)} copy(bf16[768,256]{1,0:T(8,128)(2,1)S(1)} %shard_map.118) | data formatting | bytes 786432

commit v6 on v5

--- a/solution.py
+++ b/solution.py
@@ -291,12 +291,18 @@
     sums = jnp.sum(mine, axis=0, keepdims=True)
     squares = jnp.sum(mine * mine, axis=0, keepdims=True)
 
+    early = lax.rem(gy, 2) == 0
+
     def totals_of(c):
         return lambda sel: total_split[c][sel]
 
     for c in range(parts):
         receive(0, c)
-        spread(1, c, totals_of(c))
+
+        @pl.when(early)
+        def _():
+            spread(1, c, totals_of(c))
+
         value = value + split_neigh(c, wn1)
     first[own_n:rows_n, :] = value
     sums = sums + jnp.sum(value, axis=0, keepdims=True)
@@ -312,6 +318,12 @@
     z_out[...] = total
     for j in range(1, group):
         zs_copy(j).start()
+
+    @pl.when(jnp.logical_not(early))
+    def _():
+        for c in range(parts):
+            spread(1, c, totals_of(c))
+
     for j in range(1, group):
         zs_copy(j).wait_recv()
         total = total + z_in[j - 1]

time: 37.4 us -> 37.3 us (level)
  no operation moved by 1% of the time
where the time goes in v6:
time: 37.3 us; the launch traced here: 37.1 us
  Pallas kernels  36.4 us (98%)
  local copies, waits for them, and re-layouts  0.75 us (2%)
    pallas_call x1, Pallas kernels, per_device(): call(*(pltpu.with_memory_space_constraint(x, pltpu.HBM) for x in operands))  36.4 us
    unnamed x1, local copies, waits for them, and re-layouts  0.75 us

profile of v6, /device:TPU:0, one launch (start us, length us, event | category | flops | bytes accessed | tf_op | source)
XLA Modules:
  0.0 37.1 jit_solution(8955768552351330620)
XLA Ops:
  0.0 36.4 %shard_map.118 = bf16[768,256]{1,0:T(8,128)(2,1)S(1)} custom-call(s32[8,8]{1,0:T(8,128)} %columns_hbm.1, s32[8,8]{1,0:T(8,128)} %present_hbm.1, s32[8]{0:T(128)} %root_hbm.1, s32[8]{0:T(128)} %block_hbm.1, bf16[6,128,256]{2,1,0:T(8,128)(2,1)} %bitcast.3, bf16[8,8,128,128]{3,2,1,0:T(8,128)(2,1)} %tiles_hbm.1, bf16[256,256]{1,0:T(8,128)(2,1)} %self_one_hbm.1, ...), custom_call_target="tpu_custom_call" | custom-call | tf_op jit(solution)/shard_map/pallas_call | solution.py:448
  36.4 0.7 %copy.14 = bf16[768,256]{1,0:T(8,128)(2,1)} copy(bf16[768,256]{1,0:T(8,128)(2,1)S(1)} %shard_map.118) | data formatting | bytes 786432

commit v7 on v6

--- a/solution.py
+++ b/solution.py
@@ -312,17 +312,18 @@
     xy_out[...] = total
     for n in range(len(spots)):
         xy_copy(n).start()
+
+    @pl.when(jnp.logical_not(early))
+    def _():
+        for c in range(parts):
+            spread(1, c, totals_of(c))
+
     for n in range(len(spots)):
         xy_copy(n).wait_recv()
         total = total + xy_in[n]
     z_out[...] = total
     for j in range(1, group):
         zs_copy(j).start()
-
-    @pl.when(jnp.logical_not(early))
-    def _():
-        for c in range(parts):
-            spread(1, c, totals_of(c))
 
     for j in range(1, group):
         zs_copy(j).wait_recv()

time: 37.3 us -> 36.4 us (0.976)
  Pallas kernels: 36.4 us -> 35.5 us
    pallas_call x1, Pallas kernels: 36.4 us -> 35.5 us  [per_device(): call(*(pltpu.with_memory_space_constraint(x, pltpu.HBM) for x in operands))]
where the time goes in v7:
time: 36.4 us; the launch traced here: 36.3 us
  Pallas kernels  35.5 us (98%)
  local copies, waits for them, and re-layouts  0.75 us (2%)
    pallas_call x1, Pallas kernels, per_device(): call(*(pltpu.with_memory_space_constraint(x, pltpu.HBM) for x in operands))  35.5 us
    unnamed x1, local copies, waits for them, and re-layouts  0.75 us

profile of v7, /device:TPU:0, one launch (start us, length us, event | category | flops | bytes accessed | tf_op | source)
XLA Modules:
  0.0 36.3 jit_solution(15710112805488764748)
XLA Ops:
  0.0 35.5 %shard_map.118 = bf16[768,256]{1,0:T(8,128)(2,1)S(1)} custom-call(s32[8,8]{1,0:T(8,128)} %columns_hbm.1, s32[8,8]{1,0:T(8,128)} %present_hbm.1, s32[8]{0:T(128)} %root_hbm.1, s32[8]{0:T(128)} %block_hbm.1, bf16[6,128,256]{2,1,0:T(8,128)(2,1)} %bitcast.3, bf16[8,8,128,128]{3,2,1,0:T(8,128)(2,1)} %tiles_hbm.1, bf16[256,256]{1,0:T(8,128)(2,1)} %self_one_hbm.1, ...), custom_call_target="tpu_custom_call" | custom-call | tf_op jit(solution)/shard_map/pallas_call | solution.py:449
  35.5 0.7 %copy.14 = bf16[768,256]{1,0:T(8,128)(2,1)} copy(bf16[768,256]{1,0:T(8,128)(2,1)S(1)} %shard_map.118) | data formatting | bytes 786432
